TPU v7x, 32 devices: a whole 2x2x4 slice. The times are simulated.
32 devices in a mesh: xi: 4 (over z), eta: 2 (over y), zeta: 4 (over x, core).
Axes of the slice: x: 2, y: 2, z: 4, core: 2. Of those that a mesh axis runs over, the one named last changes fastest.
Arguments:
- residual: float32 [5, 32, 32, 256], P(None, 'zeta', 'xi', 'eta'), may hold values from -6 to 6
- flow_state: float32 [5, 32, 32, 256], P(None, 'zeta', 'xi', 'eta'), may hold values from -6 to 6
- factors_zeta: float32 [3, 5, 32, 32, 256], P(None, None, 'zeta', 'xi', 'eta'), may hold values from -1.5 to 1.5, as said below
- factors_eta: float32 [3, 5, 32, 32, 256], P(None, None, 'zeta', 'xi', 'eta'), may hold values from -1.5 to 1.5, as said below
- factors_xi: float32 [3, 5, 32, 32, 256], P(None, None, 'zeta', 'xi', 'eta'), may hold values from -1.5 to 1.5, as said below
Outputs:
- update: float32 [5, 32, 32, 256], P(None, 'zeta', 'xi', 'eta')
Inputs may be any that keep to these rules, and one draw needn't show every extreme that they name: `factors_zeta`: F[g,2] is positive; the operator of each line is nonsingular. `factors_eta`: F[g,2] is positive; the operator of each line is nonsingular. `factors_xi`: F[g,2] is positive; the operator of each line is nonsingular.
All inputs are finite; a program needn't handle non-finite values.
Results may differ from a plain program's by a relative error of at most 0.000053.
Values sent between devices are 32-bit elements; how exact they have to be, the bound alone decides.
A program may use at most 128 MiB of HBM per device.

v0:
```python
import functools

import jax
import jax.numpy as jnp
from jax import lax
from jax.experimental import pallas as pl
from jax.experimental.pallas import tpu as pltpu
from jax.sharding import PartitionSpec as P

field_group = (0, 0, 0, 1, 2)
dissipation = 0.05
sublanes = 8
MESH = pl.DeviceIdType.MESH


line_order = (0, 3, 1, 4, 2)


def field_spread(own):
    return lambda planes: jnp.concatenate([planes[field_group[f]][None] for f in own], 0)


def streams_of(per_tile):
    return [own for own in (line_order[:per_tile], line_order[per_tile:]) if own]


def line_tiles(per_tile):
    distinct, uses = [], []
    for start in range(0, len(line_order), per_tile):
        groups = [field_group[f] for f in line_order[start : start + per_tile]]
        for number, have in enumerate(distinct):
            if have[: len(groups)] == groups:
                break
        else:
            number = len(distinct)
            distinct.append(groups + [groups[-1]] * (per_tile - len(groups)))
        uses.append(number)
    return distinct, uses


def forward_sweep(steps, factor, value, recent, before):
    rows = []
    for s in range(steps):
        now = -(factor(1, s) * before) if value is None else value(s) - factor(1, s) * before
        now = now - factor(0, s) * recent
        rows.append(now)
        recent, before = now, recent
    return rows


def backward_sweep(steps, factor, value, recent, before, keep):
    rows = [None] * steps
    for s in reversed(range(steps)):
        now = factor(2, s) * value(s) - factor(4, s) * before - factor(3, s) * recent
        rows[s] = now
        keep(s, now)
        recent, before = now, recent
    return rows


def responses(steps, factor, keep):
    one = jnp.ones_like(factor(0, 0))
    zero = jnp.zeros_like(one)
    lift = lambda k, s: factor(k, s)[None]
    forward = forward_sweep(
        steps, lift, None, jnp.stack([one, zero]), jnp.stack([zero, one])
    )
    none = jnp.zeros((2,) + one.shape, jnp.float32)
    backward = backward_sweep(
        steps,
        lift,
        lambda s: jnp.concatenate([forward[s], none], 0),
        jnp.stack([zero, zero, one, zero]),
        jnp.stack([zero, zero, zero, one]),
        keep,
    )
    return jnp.concatenate([forward[-1], forward[-2], backward[0], backward[1]], 0)


def chain(count, matrices, offsets, into, closed):
    c1, c2, d1, d2 = into
    entered = []
    for q in range(count):
        entered.append((c1, c2))
        if q < count - 1 or not closed:
            m, o = matrices(q), offsets(q)
            n1, n2 = m[0] * c1 + m[1] * c2, m[2] * c1 + m[3] * c2
            c1, c2 = (n1, n2) if o is None else (o[0] + n1, o[1] + n2)
    out = (c1, c2)
    result = [None] * count
    for q in reversed(range(count)):
        c1, c2 = entered[q]
        result[q] = (c1, c2, d1, d2)
        if q > 0 or not closed:
            m, o = matrices(q), offsets(q)
            n1, n2 = m[4] * c1 + m[5] * c2, m[8] * c1 + m[9] * c2
            if o is not None:
                n1, n2 = o[2] + n1, o[3] + n2
            d1, d2 = n1 + (m[6] * d1 + m[7] * d2), n2 + (m[10] * d1 + m[11] * d2)
    return result, out + (d1, d2)


class Exchange:
    def __init__(self, axis, count, send_sem, recv_sem):
        self.axis, self.count = axis, count
        self.send_sem, self.recv_sem = send_sem, recv_sem
        self.me = lax.axis_index(axis)

    def peers(self):
        return [lax.rem(self.me + k, self.count) for k in range(1, self.count)]

    def copy(self, kind, source, slots, p, slot, cut):
        pick = (lambda ref: ref) if cut is None else (lambda ref: ref.at[cut[0] : cut[1]])
        return pltpu.make_async_remote_copy(
            src_ref=pick(source(p)),
            dst_ref=pick(slots.at[slot]),
            send_sem=self.send_sem.at[kind, p],
            recv_sem=self.recv_sem.at[kind, slot],
            device_id={self.axis: p},
            device_id_type=MESH,
        )

    def start(self, kind, source, slots, cut=None, sends=None):
        for p in self.peers():
            go = lambda p=p: self.copy(kind, source, slots, p, self.me, cut).start()
            go() if sends is None else pl.when(sends(self.me, p))(go)

    def wait_recv(self, kind, source, slots, cut=None, sends=None):
        for p in self.peers():
            go = lambda p=p: self.copy(kind, source, slots, p, p, cut).wait_recv()
            go() if sends is None else pl.when(sends(p, self.me))(go)

    def wait_send(self, kind, source, slots, cut=None, sends=None):
        for p in self.peers():
            go = lambda p=p: self.copy(kind, source, slots, p, self.me, cut).wait_send()
            go() if sends is None else pl.when(sends(self.me, p))(go)


class Split:
    def __init__(self, exchange, lift, m_send, m_slots, o_send, o_slots, r_send, r_slots, full):
        self.x, self.lift = exchange, lift
        self.m_send, self.m_slots = m_send, m_slots
        self.o_send, self.o_slots = o_send, o_slots
        self.r_send, self.r_slots, self.full = r_send, r_slots, full
        self.parts = m_send.shape[0]
        self.rows = sublanes // self.parts
        pick = (lambda p: p) if self.parts > 1 else (lambda p: 0)
        last = exchange.count - 1
        m_from = lambda p: m_send.at[pick(p)]
        o_from = lambda p: o_send.at[pick(p)]
        r_from = lambda p: r_send.at[p]
        self.matrices = (0, m_from, m_slots)
        self.ahead = (1, o_from, o_slots, (0, 2), lambda a, b: a < last)
        self.behind = (2, o_from, o_slots, (2, 4), lambda a, b: a > 0)
        self.carried = (3, r_from, r_slots, (0, 2), lambda a, b: b > 0)
        self.returned = (4, r_from, r_slots, (2, 4), lambda a, b: b < last)
        self.pick = pick

    def clear_ends(self):
        if self.parts > 1:
            nothing = jnp.zeros((self.parts, 2) + self.r_slots.shape[2:], jnp.float32)

            @pl.when(self.x.me == 0)
            def _():
                self.r_slots[:, 0:2] = nothing

            @pl.when(self.x.me == self.x.count - 1)
            def _():
                self.r_slots[:, 2:4] = nothing

    def put(self, route, value, send, slots, lo):
        hi = lo + value.shape[0]
        for p in range(self.parts):
            send[p, lo:hi] = value[:, :, p * self.rows : (p + 1) * self.rows, :]
        slots[self.x.me, lo:hi] = send[self.pick(self.x.me), lo:hi]
        self.x.start(*route)

    def put_matrices(self, value):
        self.put(self.matrices, value, self.m_send, self.m_slots, 0)

    def put_ahead(self, value):
        self.put(self.ahead, value, self.o_send, self.o_slots, 0)

    def put_behind(self, value):
        self.put(self.behind, value, self.o_send, self.o_slots, 2)

    def solve(self):
        x = self.x
        for route in (self.matrices, self.ahead, self.behind):
            x.wait_recv(*route)
        zero = jnp.zeros(self.o_slots.shape[2:], jnp.float32)
        solved, _ = chain(
            x.count,
            lambda q: [self.lift(self.m_slots[q, k]) for k in range(12)],
            lambda q: [self.o_slots[q, k] for k in range(4)],
            (zero,) * 4,
            True,
        )
        for q, planes in enumerate(solved):
            for k in range(4):
                self.r_send[q, k] = planes[k]
        if self.parts > 1:
            x.start(*self.carried)
            x.start(*self.returned)
            me = x.me

            @pl.when(me > 0)
            def _():
                self.r_slots[me, 0:2] = self.r_send[me, 0:2]

            @pl.when(me < x.count - 1)
            def _():
                self.r_slots[me, 2:4] = self.r_send[me, 2:4]

    def result(self):
        x = self.x
        if self.parts == 1:
            return [self.r_send[x.me, k] for k in range(4)]
        x.wait_recv(*self.carried)
        x.wait_recv(*self.returned)
        for p in range(self.parts):
            self.full[:, :, p * self.rows : (p + 1) * self.rows, :] = self.r_slots[p]
        return [self.full[k] for k in range(4)]

    def finish(self):
        for route in (self.matrices, self.ahead, self.behind):
            self.x.wait_send(*route)
        if self.parts > 1:
            self.x.wait_send(*self.carried)
            self.x.wait_send(*self.returned)


def times(m, v):
    return m[0] * v[0] + m[1] * v[1], m[2] * v[0] + m[3] * v[1]


def plus(a, b):
    return a[0] + b[0], a[1] + b[1]


class Pairs:
    def __init__(self, exchange, lifts, m_own, m_in, g_own, g_in, streams, ss, rs):
        self.axis, self.me, self.lifts = exchange.axis, exchange.me, lifts
        self.m_own, self.m_in, self.g_own, self.g_in = m_own, m_in, g_own, g_in
        self.streams = streams
        ahead, behind, top, mid = (slice(0, 2), slice(2, 4), slice(0, 4), slice(4, 8))
        cut = lambda a, b, part: (a.at[part], b.at[part])
        self.messages = [
            (0, 1, 0, m_own, m_in),
            (0, 3, 2, *cut(m_own, m_in, mid)),
            (0, 2, 3, *cut(m_own, m_in, top)),
            (1, 2, 1, g_own, g_in),
            (1, 2, 0, g_own, g_in),
        ]
        for h, (o_own, o_in, j_own, j_in, _) in enumerate(streams):
            kind = 2 + 3 * h
            self.messages += [
                (kind, 0, 1, *cut(o_own, o_in, ahead)),
                (kind, 1, 0, *cut(o_own, o_in, ahead)),
                (kind, 2, 3, *cut(o_own, o_in, ahead)),
                (kind + 1, 1, 0, *cut(o_own, o_in, behind)),
                (kind + 1, 3, 2, *cut(o_own, o_in, behind)),
                (kind + 2, 1, 2, j_own, j_in),
                (kind + 2, 1, 3, j_own, j_in),
                (kind + 2, 2, 1, j_own, j_in),
                (kind + 2, 2, 0, j_own, j_in),
            ]
        self.ss, self.rs = ss, rs

    def copy(self, message):
        kind, _, to, source, destination = message
        return pltpu.make_async_remote_copy(
            src_ref=source,
            dst_ref=destination,
            send_sem=self.ss.at[kind, to],
            recv_sem=self.rs.at[kind],
            device_id={self.axis: to},
            device_id_type=MESH,
        )

    def role(self, number):
        return pl.when(self.me == number)

    def start(self, kind, number):
        for message in self.messages:
            if message[0] == kind and message[1] == number:
                self.copy(message).start()

    def start_all(self, kind):
        for number in range(4):
            if any(m[0] == kind and m[1] == number for m in self.messages):
                self.role(number)(lambda number=number: self.start(kind, number))

    def wait(self, kind, number):
        for message in self.messages:
            if message[0] == kind and message[2] == number:
                self.copy(message).wait_recv()

    def clear_ends(self):
        pass

    def put_matrices(self, value):
        for place, k in enumerate((0, 1, 2, 3, 4, 5, 8, 9, 6, 7, 10, 11)):
            self.m_own[place] = value[k]
        self.start_all(0)

    def join_matrices(self):
        @self.role(2)
        def _():
            self.wait(0, 2)
            own = [self.m_own[k] for k in range(12)]
            far = [self.m_in[4 + k] for k in range(4)]
            columns = []
            for j in range(2):
                through = times(far, (own[j], own[2 + j]))
                columns.append(plus((own[4 + j], own[6 + j]), times(own[8:12], through)))
            for i in range(2):
                for j in range(2):
                    self.g_own[2 * i + j] = columns[j][i]
            self.start(1, 2)

    def put_ahead(self, h, value):
        self.streams[h][0][0:2] = value
        self.start_all(2 + 3 * h)

    def put_behind(self, h, value):
        self.streams[h][0][2:4] = value
        self.start_all(3 + 3 * h)

    def solve(self, h):
        o_own, o_in, j_own, j_in, full = self.streams[h]
        kind = 2 + 3 * h
        lifted = lambda ref, lo: [self.lifts[h](ref[k]) for k in range(lo, lo + 4)]

        @self.role(1)
        def _():
            self.wait(kind, 1)
            c = plus((o_own[0], o_own[1]), times(lifted(self.m_own, 0), (o_in[0], o_in[1])))
            j_own[0], j_own[1] = c
            self.start(kind + 2, 1)

        @self.role(2)
        def _():
            self.wait(kind + 1, 2)
            far = plus((o_in[2], o_in[3]), times(lifted(self.m_in, 4), (o_own[0], o_own[1])))
            g = plus((o_own[2], o_own[3]), times(lifted(self.m_own, 8), far))
            j_own[0], j_own[1] = g
            self.start(kind + 2, 2)

    def result(self, h):
        o_own, o_in, j_own, j_in, full = self.streams[h]
        kind = 2 + 3 * h
        lifted = lambda ref, lo: [self.lifts[h](ref[k]) for k in range(lo, lo + 4)]
        pair = lambda ref, k: (ref[k], ref[k + 1])
        zero = jnp.zeros(full.shape[1:], jnp.float32)

        def store(c, d):
            for k, plane in enumerate((*c, *d)):
                full[k] = plane

        def wait(number, once, kinds):
            for k in (once if h == 0 else ()) + kinds:
                self.wait(k, number)

        @self.role(0)
        def _():
            wait(0, (0, 1), (kind, kind + 1, kind + 2))
            c1 = pair(o_own, 0)
            c2 = plus(pair(o_in, 0), times(lifted(self.m_in, 0), c1))
            d1 = plus(pair(j_in, 0), times(lifted(self.g_in, 0), c2))
            d0 = plus(pair(o_in, 2), times(lifted(self.m_in, 4), c1))
            store((zero, zero), plus(d0, times(lifted(self.m_in, 8), d1)))

        @self.role(1)
        def _():
            wait(1, (1,), (kind + 2,))
            store(
                pair(o_in, 0), plus(pair(j_in, 0), times(lifted(self.g_in, 0), pair(j_own, 0)))
            )

        @self.role(2)
        def _():
            wait(2, (), (kind + 2,))
            c2 = pair(j_in, 0)
            c3 = plus(pair(o_own, 0), times(lifted(self.m_own, 0), c2))
            store(c2, plus(pair(o_in, 2), times(lifted(self.m_in, 4), c3)))

        @self.role(3)
        def _():
            wait(3, (0,), (kind, kind + 2))
            c3 = plus(pair(o_in, 0), times(lifted(self.m_in, 0), pair(j_in, 0)))
            store(c3, (zero, zero))

        return [full[k] for k in range(4)]

    def finish(self):
        for number in range(4):

            @self.role(number)
            def _(number=number):
                for message in self.messages:
                    if message[1] == number:
                        self.copy(message).wait_send()


class Splits:
    def __init__(self, exchange, lifts, scratch):
        self.each = []
        for lift, (*buffers, ss, rs) in zip(lifts, scratch):
            own = Exchange(exchange.axis, exchange.count, ss, rs)
            self.each.append(Split(own, lift, *buffers))

    def clear_ends(self):
        for one in self.each:
            one.clear_ends()

    def put_matrices(self, value):
        for one in self.each:
            one.put_matrices(value)

    def join_matrices(self):
        pass

    def put_ahead(self, h, value):
        self.each[h].put_ahead(value)

    def put_behind(self, h, value):
        self.each[h].put_behind(value)

    def solve(self, h):
        self.each[h].solve()

    def result(self, h):
        return self.each[h].result()

    def finish(self):
        for one in self.each:
            one.finish()


def solver(exchange, lifts, scratch):
    if exchange.count == 4:
        return Pairs(exchange, lifts, *scratch)
    return Splits(exchange, lifts, scratch)


def corrected(local, response, incoming, lift):
    total = local
    for k in range(4):
        total = total + lift(response[k]) * incoming[k]
    return total


def kernel(
    counts, residual_hbm, flow_hbm, f_zeta_hbm, f_eta_hbm, f_xi_hbm, out,
    residual, flow, f_zeta, f_eta, f_xi, in_sem,
    z_scratch, x_scratch, e_streams, e_matrices, e_msend, e_mslots, e_inner, e_ss, e_rs,
    z_response, x_response, e_response, x_factors, e_factors, lines, turned, turned_factors,
    hz, hx_send, hx, he_send, he, padded, source, h_ss, h_rs,
):
    n_xi, n_eta, n_zeta = counts
    fields, cz, cx, cy = flow.shape
    planes = fields * cz
    xz = Exchange("zeta", n_zeta, None, None)
    xe = Exchange("eta", n_eta, e_ss, e_rs)
    xx = Exchange("xi", n_xi, None, None)
    per_tile = cy // (cz * cx)
    streams = streams_of(per_tile)
    lifts = [field_spread(own) for own in streams]
    zeta = solver(xz, lifts, z_scratch)
    xi = solver(xx, lifts, x_scratch)

    barrier = pltpu.get_barrier_semaphore()
    greeted = 0
    for x in (xz, xe, xx):
        for p in x.peers():
            pl.semaphore_signal(barrier, inc=1, device_id={x.axis: p}, device_id_type=MESH)
            greeted += 1

    loads = [
        pltpu.make_async_copy(src, dst, in_sem.at[k])
        for k, (src, dst) in enumerate(
            (
                (flow_hbm, flow),
                (f_zeta_hbm, f_zeta),
                (f_xi_hbm, f_xi),
                (residual_hbm, residual),
                (f_eta_hbm, f_eta),
            )
        )
    ]
    for load in loads:
        load.start()
    zeta.clear_ends()
    xi.clear_ends()
    loads[0].wait()

    per_pack = cy // 4
    lane = lax.broadcasted_iota(jnp.int32, (cx, cy), 1)
    packs = [jnp.zeros((cx, cy), jnp.float32) for _ in range(he_send.shape[0])]
    eta_part = []
    for k in range(planes):
        at = k % per_pack
        v = flow[k // cz, k % cz]
        up1, up2 = pltpu.roll(v, 1, 1), pltpu.roll(v, 2, 1)
        down1, down2 = pltpu.roll(v, cy - 1, 1), pltpu.roll(v, cy - 2, 1)
        near_low, near_high = lane < 1, lane >= cy - 1
        far_low, far_high = lane < 2, lane >= cy - 2
        near = jnp.where(near_low, 0.0, up1) + jnp.where(near_high, 0.0, down1)
        far = jnp.where(far_low, 0.0, up2) + jnp.where(far_high, 0.0, down2)
        eta_part.append(far - 4.0 * near)
        near = jnp.where(near_low, up1, jnp.where(near_high, down1, 0.0))
        far = jnp.where(far_low, up2, jnp.where(far_high, down2, 0.0))
        face = -dissipation * (far - 4.0 * near)
        moved = pltpu.roll(face, (4 * at + 2) % cy, 1)
        packs[k // per_pack] = jnp.where(lane // 4 == at, moved, packs[k // per_pack])
    for k, pack in enumerate(packs):
        he_send[k] = pack
    row = lambda x: flow[:, :, x : x + 1, :]
    hx_send[0, :, :, 0:1, :] = -dissipation * (row(cx - 2) - 4.0 * row(cx - 1))
    hx_send[0, :, :, 1:2, :] = -dissipation * row(cx - 1)
    hx_send[1, :, :, 0:1, :] = -dissipation * row(0)
    hx_send[1, :, :, 1:2, :] = -dissipation * (row(1) - 4.0 * row(0))

    pl.semaphore_wait(barrier, greeted)

    halos = (
        (xx, hx, lambda side: hx_send.at[side]),
        (xe, he, lambda side: he_send),
        (xz, hz, lambda side: flow.at[:, cz - 2 : cz] if side == 0 else flow.at[:, 0:2]),
    )

    def halo_copy(number, side):
        x, slots, origin = halos[number]
        step = 1 if side == 0 else x.count - 1
        return pltpu.make_async_remote_copy(
            src_ref=origin(side),
            dst_ref=slots.at[side],
            send_sem=h_ss.at[number, side],
            recv_sem=h_rs.at[number, side],
            device_id={x.axis: lax.rem(x.me + step, x.count)},
            device_id_type=MESH,
        )

    for number, (x, slots, origin) in enumerate(halos):
        for side in range(2):
            sends = x.me < x.count - 1 if side == 0 else x.me > 0
            has = x.me > 0 if side == 0 else x.me < x.count - 1
            pl.when(sends)(lambda number=number, side=side: halo_copy(number, side).start())

            @pl.when(jnp.logical_not(has))
            def _(slots=slots, side=side):
                slots[side] = jnp.zeros(slots.shape[1:], jnp.float32)

    loads[1].wait()

    def keep_z(s, now):
        z_response[s] = now

    zeta.put_matrices(responses(cz, lambda k, s: f_zeta[:, k, s], keep_z))

    state = flow[...]
    nothing = jnp.zeros((fields, cz, 2, cy), jnp.float32)
    padded[:, :, 8 - 2 : 8, :] = nothing
    padded[:, :, 8 : 8 + cx, :] = state
    padded[:, :, 8 + cx : 8 + cx + 2, :] = nothing
    none = jnp.zeros((fields, 2, cx, cy), jnp.float32)
    long = jnp.concatenate([none, state, none], 1)
    near = (padded[:, :, 7 : 7 + cx, :] + padded[:, :, 9 : 9 + cx, :]) + (
        long[:, 1 : 1 + cz] + long[:, 3 : 3 + cz]
    )
    far = (padded[:, :, 6 : 6 + cx, :] + padded[:, :, 10 : 10 + cx, :]) + (
        long[:, 0:cz] + long[:, 4 : 4 + cz]
    )
    total_part = 18.0 * state - 4.0 * near + far + jnp.stack(eta_part).reshape(flow.shape)
    loads[3].wait()
    source[...] = residual[...] - dissipation * total_part

    loads[2].wait()

    for s in range(cx):
        for k in range(5):
            for g in range(3):
                x_factors[k, s, g] = f_xi[pl.ds((g * 5 + k) * cz * cx + s, cz, stride=cx), :]

    def xi_factor(k, s):
        return x_factors[k, s]

    def keep_x(s, now):
        x_response[s] = now

    xi.put_matrices(responses(cx, xi_factor, keep_x))
    zeta.join_matrices()

    for number, (x, slots, origin) in enumerate(halos):
        for side in range(2):
            has = x.me > 0 if side == 0 else x.me < x.count - 1
            pl.when(has)(lambda number=number, side=side: halo_copy(number, side).wait_recv())

    source[:, :, 0:2, :] += hx[0]
    source[:, :, cx - 2 : cx, :] += hx[1]
    zeta_faces = {
        0: hz[0, :, 0] - 4.0 * hz[0, :, 1],
        1: hz[0, :, 1],
        cz - 2: hz[1, :, 0],
        cz - 1: hz[1, :, 1] - 4.0 * hz[1, :, 0],
    }
    faces = [jnp.where(lane % 4 >= 2, he[0, k], he[1, k]) for k in range(he.shape[1])]
    edge = jnp.logical_or(lane < 2, lane >= cy - 2)

    def eta_face(f, z):
        k = f * cz + z
        back = (cy - (4 * (k % per_pack) + 2)) % cy
        return jnp.where(edge, pltpu.roll(faces[k // per_pack], back, 1), 0.0)

    def source_plane(own, z):
        value = jnp.stack([source[f, z] + eta_face(f, z) for f in own])
        if z in zeta_faces:
            value = value - dissipation * jnp.stack([zeta_faces[z][f] for f in own])
        return value

    z_local = []
    for h, own in enumerate(streams):
        z_factor = lambda k, s: lifts[h](f_zeta[:, k, s])
        zero = jnp.zeros((len(own), cx, cy), jnp.float32)
        forward = forward_sweep(cz, z_factor, lambda s: source_plane(own, s), zero, zero)
        zeta.put_ahead(h, jnp.stack([forward[-1], forward[-2]]))
        local = backward_sweep(
            cz, z_factor, lambda s: forward[s], zero, zero, lambda s, now: None
        )
        zeta.put_behind(h, jnp.stack([local[0], local[1]]))
        z_local.append(local)
    for h in range(len(streams)):
        zeta.solve(h)

    loads[4].wait()
    tiles = lines.shape[0] // cy
    steps = cy // sublanes
    total = lines.shape[0]
    distinct, uses = line_tiles(cy // (cz * cx))
    for k in range(5):
        for t, groups in enumerate(distinct):
            whole = jnp.concatenate([f_eta[g * 5 + k] for g in groups], 0)
            turned_factors[t * cy : (t + 1) * cy, :] = whole.T
        for s in range(steps):
            e_factors[k, s] = turned_factors[
                pl.ds(s, len(distinct) * sublanes, stride=steps), :
            ].reshape(len(distinct), sublanes, cy)

    def tiled(planes, at=slice(None)):
        return jnp.concatenate([planes[u : u + 1] for u in uses[at]], 0)

    xi.join_matrices()

    def eta_factor(k, s):
        return e_factors[k, s]

    def keep_e(s, now):
        e_response[s] = now

    e_matrices[...] = responses(steps, eta_factor, keep_e)
    chunk = lambda c: [e_matrices[k, :, c : c + 1, :] for k in range(12)]
    one = jnp.ones((1, len(distinct), 1, cy), jnp.float32)
    zero = jnp.zeros_like(one)
    unit = lambda j: jnp.concatenate([one if i == j else zero for i in range(4)], 0)
    inner, left = chain(sublanes, chunk, lambda c: None, [unit(j) for j in range(4)], False)
    for c, values in enumerate(inner):
        for k in range(4):
            e_inner[k, :, :, c : c + 1, :] = values[k]
    e_msend[...] = jnp.concatenate([left[0][0:2], left[1][0:2], left[2], left[3]], 0)
    e_mslots[xe.me] = e_msend[...]
    xe.start(0, lambda p: e_msend, e_mslots)

    if total > planes * cx:
        lines[planes * cx : total, :] = jnp.zeros((total - planes * cx, cy), jnp.float32)

    def turn(source_ref, target_ref, at):
        for t in range(at.start, at.stop):
            target_ref[t * cy : (t + 1) * cy, :] = source_ref[t * cy : (t + 1) * cy, :].T

    first, parts = 0, []
    for own in streams:
        count = -(-len(own) // per_tile)
        parts.append((first, slice(first // per_tile, first // per_tile + count)))
        first += len(own)
    e_local = []
    for h, own in enumerate(streams):
        place, at = parts[h]
        count = at.stop - at.start
        incoming = zeta.result(h)
        for s in range(cz):
            done = corrected(z_local[h][s], z_response[s], incoming, lifts[h])
            for k in range(len(own)):
                row = ((place + k) * cz + s) * cx
                lines[row : row + cx, :] = done[k]
        turn(lines, turned, at)
        offsets, o_send, o_slots, results, inside = e_streams[h]
        rows = lambda s: pl.ds(at.start * cy + s, count * sublanes, stride=steps)
        zero = jnp.zeros((count, sublanes, cy), jnp.float32)
        eta_tiles = lambda k, s: tiled(e_factors[k, s], at)
        forward = forward_sweep(
            steps, eta_tiles, lambda s: turned[rows(s), :].reshape(zero.shape), zero, zero
        )
        local = backward_sweep(
            steps, eta_tiles, lambda s: forward[s], zero, zero, lambda s, now: None
        )
        e_local.append(local)
        for k, value in enumerate((forward[-1], forward[-2], local[0], local[1])):
            offsets[k] = value
        none = jnp.zeros((count, 1, cy), jnp.float32)
        inner, left = chain(
            sublanes,
            lambda c: [tiled(plane, at) for plane in chunk(c)],
            lambda c: [offsets[k, :, c : c + 1, :] for k in range(4)],
            (none,) * 4,
            False,
        )
        for k in range(4):
            o_send[k] = left[k]
        o_slots[xe.me] = o_send[...]
        xe.start(1 + h, lambda p: o_send, o_slots)
        for c, values in enumerate(inner):
            for k in range(4):
                inside[k, :, c : c + 1, :] = values[k]

    x_local = []
    for h, own in enumerate(streams):
        place, at = parts[h]
        count = at.stop - at.start
        offsets, o_send, o_slots, results, inside = e_streams[h]
        if h == 0:
            xe.wait_recv(0, lambda p: e_msend, e_mslots)
        xe.wait_recv(1 + h, lambda p: o_send, o_slots)
        none = jnp.zeros((count, 1, cy), jnp.float32)
        solved, _ = chain(
            n_eta,
            lambda q: [tiled(e_mslots[q, k], at) for k in range(12)],
            lambda q: [o_slots[q, k] for k in range(4)],
            (none,) * 4,
            True,
        )
        for q, values in enumerate(solved):
            for k in range(4):
                results[q, k] = values[k]
        enters = [results[xe.me, k] for k in range(4)]
        incoming = []
        for k in range(4):
            value = inside[k]
            for j in range(2 if k < 2 else 4):
                value = value + tiled(e_inner[k, j], at) * enters[j]
            incoming.append(value)
        rows = lambda s: pl.ds(at.start * cy + s, count * sublanes, stride=steps)
        for s in range(steps):
            done = corrected(e_local[h][s], e_response[s], incoming, lambda r: tiled(r, at))
            turned[rows(s), :] = done.reshape(count * sublanes, cy)
        turn(turned, lines, at)
        x_factor = lambda k, s: lifts[h](xi_factor(k, s))
        zero = jnp.zeros((len(own), cz, cy), jnp.float32)
        columns = lambda s: pl.ds(place * cz * cx + s, len(own) * cz, stride=cx)
        forward = forward_sweep(
            cx, x_factor, lambda s: lines[columns(s), :].reshape(zero.shape), zero, zero
        )
        xi.put_ahead(h, jnp.stack([forward[-1], forward[-2]]))
        local = backward_sweep(
            cx, x_factor, lambda s: forward[s], zero, zero, lambda s, now: None
        )
        xi.put_behind(h, jnp.stack([local[0], local[1]]))
        x_local.append(local)
    for h in range(len(streams)):
        xi.solve(h)
    for h, own in enumerate(streams):
        incoming = xi.result(h)
        for s in range(cx):
            done = corrected(x_local[h][s], x_response[s], incoming, lifts[h])
            for k, f in enumerate(own):
                out[pl.ds(f * cz * cx + s, cz, stride=cx), :] = done[k]

    zeta.finish()
    xi.finish()
    xe.wait_send(0, lambda p: e_msend, e_mslots)
    for h, (_, o_send, o_slots, _, _) in enumerate(e_streams):
        xe.wait_send(1 + h, lambda p: o_send, o_slots)
    for number, (x, slots, origin) in enumerate(halos):
        for side in range(2):
            sends = x.me < x.count - 1 if side == 0 else x.me > 0
            pl.when(sends)(lambda number=number, side=side: halo_copy(number, side).wait_send())


def solver_scratch(count, streams, lanes):
    vmem = lambda *shape: pltpu.VMEM(shape, jnp.float32)
    dma = pltpu.SemaphoreType.DMA
    if count == 4:
        plane = (sublanes, lanes)
        return (
            vmem(12, 3, *plane),
            vmem(12, 3, *plane),
            vmem(4, 3, *plane),
            vmem(4, 3, *plane),
            tuple(
                tuple(vmem(n, len(own), *plane) for n in (4, 4, 2, 2, 4)) for own in streams
            ),
            dma((2 + 3 * len(streams), count)),
            dma((2 + 3 * len(streams),)),
        )
    parts = count if sublanes % count == 0 else 1
    rows = sublanes // parts
    return tuple(
        (
            vmem(parts, 12, 3, rows, lanes),
            vmem(count, 12, 3, rows, lanes),
            vmem(parts, 4, len(own), rows, lanes),
            vmem(count, 4, len(own), rows, lanes),
            vmem(count, 4, len(own), rows, lanes),
            vmem(count, 4, len(own), rows, lanes),
            vmem(4, len(own), sublanes, lanes),
            dma((5, count)),
            dma((5, count)),
        )
        for own in streams
    )


def on_device(counts, residual, flow_state, factors_zeta, factors_eta, factors_xi):
    n_xi, n_eta, n_zeta = counts
    fields, cz, cx, cy = flow_state.shape
    total = -(-(fields * cz * cx) // cy) * cy
    tiles = total // cy
    steps = cy // sublanes
    packs = -(-(fields * cz) // (cy // 4))
    distinct = len(line_tiles(cy // (cz * cx))[0])
    vmem = lambda *shape: pltpu.VMEM(shape, jnp.float32)
    dma = pltpu.SemaphoreType.DMA
    whole = pl.BlockSpec(memory_space=pltpu.VMEM)
    per_tile = cy // (cz * cx)
    streams = streams_of(per_tile)
    eta_streams = []
    for own in streams:
        count = -(-len(own) // per_tile)
        eta_streams.append(
            (
                vmem(4, count, sublanes, cy),
                vmem(4, count, 1, cy),
                vmem(n_eta, 4, count, 1, cy),
                vmem(n_eta, 4, count, 1, cy),
                vmem(4, count, sublanes, cy),
            )
        )
    scratch = (
        [
            vmem(fields, cz, cx, cy),
            vmem(fields, cz, cx, cy),
            vmem(3, 5, cz, cx, cy),
            vmem(15, cz * cx, cy),
            vmem(15 * cz * cx, cy),
            dma((5,)),
            solver_scratch(n_zeta, streams, cy),
            solver_scratch(n_xi, streams, cy),
            tuple(eta_streams),
            vmem(12, distinct, sublanes, cy),
            vmem(12, distinct, 1, cy),
            vmem(n_eta, 12, distinct, 1, cy),
            vmem(4, 4, distinct, sublanes, cy),
            dma((1 + len(streams), n_eta)),
            dma((1 + len(streams), n_eta)),
            vmem(cz, 4, 3, cx, cy),
            vmem(cx, 4, 3, cz, cy),
            vmem(steps, 4, distinct, sublanes, cy),
            vmem(5, cx, 3, cz, cy),
            vmem(5, steps, distinct, sublanes, cy),
            vmem(total, cy),
            vmem(total, cy),
            vmem(distinct * cy, cy),
            vmem(2, fields, 2, cx, cy),
            vmem(2, fields, cz, 2, cy),
            vmem(2, fields, cz, 2, cy),
            vmem(packs, cx, cy),
            vmem(2, packs, cx, cy),
            vmem(fields, cz, cx + 16, cy),
            vmem(fields, cz, cx, cy),
            dma((3, 2)),
            dma((3, 2)),
        ]
    )
    update = pl.pallas_call(
        functools.partial(kernel, counts),
        out_shape=jax.ShapeDtypeStruct((fields * cz * cx, cy), jnp.float32),
        in_specs=[pl.BlockSpec(memory_space=pltpu.HBM)] * 5,
        out_specs=whole,
        scratch_shapes=scratch,
        compiler_params=pltpu.CompilerParams(
            collective_id=0, has_side_effects=True, vmem_limit_bytes=24 * 2**20
        ),
    )(
        *(
            pltpu.with_memory_space_constraint(operand, pltpu.HBM)
            for operand in (
                residual,
                flow_state,
                factors_zeta,
                factors_eta.reshape(15, cz * cx, cy),
                factors_xi.reshape(15 * cz * cx, cy),
            )
        )
    )
    return update.reshape(flow_state.shape)


def solution(mesh):
    fields = P(None, "zeta", "xi", "eta")
    factors = P(None, None, "zeta", "xi", "eta")
    counts = tuple(mesh.shape[axis] for axis in ("xi", "eta", "zeta"))
    return jax.shard_map(
        functools.partial(on_device, counts),
        mesh=mesh,
        in_specs=(fields, fields, factors, factors, factors),
        out_specs=fields,
        check_vma=False,
    )
```

profile of v0, /device:TPU:0, one launch (start us, length us, event | category | flops | bytes accessed | tf_op | source)
XLA Modules:
  0.0 23.6 jit_solution(3705136626195815956)
XLA Ops:
  0.0 22.9 %shard_map.55 = f32[320,128]{1,0:T(8,128)S(1)} custom-call(f32[5,8,8,128]{3,2,1,0:T(8,128)} %residual_hbm.1, f32[5,8,8,128]{3,2,1,0:T(8,128)} %flow_hbm.1, f32[3,5,8,8,128]{4,3,2,1,0:T(8,128)} %f_zeta_hbm.1, f32[15,64,128]{2,1,0:T(8,128)} %bitcast.4, f32[960,128]{1,0:T(8,128)} %bitcast.5), custom_call_target="tpu_custom_call" | custom-call | tf_op jit(solution)/shard_map/pallas_call | solution.py:884
  22.9 0.7 %copy.7 = f32[5,8,8,128]{3,2,1,0:T(8,128)} copy(f32[5,8,8,128]{3,2,1,0:T(8,128)S(1)} %bitcast.3) | data formatting | bytes 327680
where the time goes:
time: 23.7 us; the launch traced here: 23.6 us
  Pallas kernels  22.9 us (97%)
  local copies, waits for them, and re-layouts  0.67 us (3%)
    pallas_call x1, Pallas kernels, on_device(): pl.pallas_call(functools.partial(kernel, counts), out_shape=jax.ShapeDtyp...  22.9 us
    unnamed x1, local copies, waits for them, and re-layouts  0.67 us

commit v1 on v0

--- a/solution.py
+++ b/solution.py
@@ -470,13 +470,6 @@
     zeta = solver(xz, lifts, z_scratch)
     xi = solver(xx, lifts, x_scratch)
 
-    barrier = pltpu.get_barrier_semaphore()
-    greeted = 0
-    for x in (xz, xe, xx):
-        for p in x.peers():
-            pl.semaphore_signal(barrier, inc=1, device_id={x.axis: p}, device_id_type=MESH)
-            greeted += 1
-
     loads = [
         pltpu.make_async_copy(src, dst, in_sem.at[k])
         for k, (src, dst) in enumerate(
@@ -489,12 +482,55 @@
             )
         )
     ]
-    for load in loads:
+    loads[0].start()
+
+    barrier = pltpu.get_barrier_semaphore()
+    greeted = 0
+    for x in (xz, xe, xx):
+        for p in x.peers():
+            pl.semaphore_signal(barrier, inc=1, device_id={x.axis: p}, device_id_type=MESH)
+            greeted += 1
+
+    for load in loads[1:]:
         load.start()
     zeta.clear_ends()
     xi.clear_ends()
     loads[0].wait()
 
+    row = lambda x: flow[:, :, x : x + 1, :]
+    hx_send[0, :, :, 0:1, :] = -dissipation * (row(cx - 2) - 4.0 * row(cx - 1))
+    hx_send[0, :, :, 1:2, :] = -dissipation * row(cx - 1)
+    hx_send[1, :, :, 0:1, :] = -dissipation * row(0)
+    hx_send[1, :, :, 1:2, :] = -dissipation * (row(1) - 4.0 * row(0))
+
+    pl.semaphore_wait(barrier, greeted)
+
+    halos = (
+        (xx, hx, lambda side: hx_send.at[side]),
+        (xe, he, lambda side: he_send),
+        (xz, hz, lambda side: flow_hbm.at[:, cz - 2 : cz] if side == 0 else flow_hbm.at[:, 0:2]),
+    )
+
+    def halo_copy(number, side):
+        x, slots, origin = halos[number]
+        step = 1 if side == 0 else x.count - 1
+        return pltpu.make_async_remote_copy(
+            src_ref=origin(side),
+            dst_ref=slots.at[side],
+            send_sem=h_ss.at[number, side],
+            recv_sem=h_rs.at[number, side],
+            device_id={x.axis: lax.rem(x.me + step, x.count)},
+            device_id_type=MESH,
+        )
+
+    def halo_start(number):
+        x = halos[number][0]
+        for side in range(2):
+            sends = x.me < x.count - 1 if side == 0 else x.me > 0
+            pl.when(sends)(lambda side=side: halo_copy(number, side).start())
+
+    halo_start(0)
+    halo_start(2)
     per_pack = cy // 4
     lane = lax.broadcasted_iota(jnp.int32, (cx, cy), 1)
     packs = [jnp.zeros((cx, cy), jnp.float32) for _ in range(he_send.shape[0])]
@@ -516,37 +552,10 @@
         packs[k // per_pack] = jnp.where(lane // 4 == at, moved, packs[k // per_pack])
     for k, pack in enumerate(packs):
         he_send[k] = pack
-    row = lambda x: flow[:, :, x : x + 1, :]
-    hx_send[0, :, :, 0:1, :] = -dissipation * (row(cx - 2) - 4.0 * row(cx - 1))
-    hx_send[0, :, :, 1:2, :] = -dissipation * row(cx - 1)
-    hx_send[1, :, :, 0:1, :] = -dissipation * row(0)
-    hx_send[1, :, :, 1:2, :] = -dissipation * (row(1) - 4.0 * row(0))
-
-    pl.semaphore_wait(barrier, greeted)
-
-    halos = (
-        (xx, hx, lambda side: hx_send.at[side]),
-        (xe, he, lambda side: he_send),
-        (xz, hz, lambda side: flow.at[:, cz - 2 : cz] if side == 0 else flow.at[:, 0:2]),
-    )
-
-    def halo_copy(number, side):
-        x, slots, origin = halos[number]
-        step = 1 if side == 0 else x.count - 1
-        return pltpu.make_async_remote_copy(
-            src_ref=origin(side),
-            dst_ref=slots.at[side],
-            send_sem=h_ss.at[number, side],
-            recv_sem=h_rs.at[number, side],
-            device_id={x.axis: lax.rem(x.me + step, x.count)},
-            device_id_type=MESH,
-        )
-
-    for number, (x, slots, origin) in enumerate(halos):
+    halo_start(1)
+    for x, slots, origin in halos:
         for side in range(2):
-            sends = x.me < x.count - 1 if side == 0 else x.me > 0
             has = x.me > 0 if side == 0 else x.me < x.count - 1
-            pl.when(sends)(lambda number=number, side=side: halo_copy(number, side).start())
 
             @pl.when(jnp.logical_not(has))
             def _(slots=slots, side=side):

time: 23.7 us -> 23.9 us (level)
  no operation moved by 1% of the time
where the time goes in v1:
time: 23.9 us; the launch traced here: 23.8 us
  Pallas kernels  23.1 us (97%)
  local copies, waits for them, and re-layouts  0.67 us (3%)
    pallas_call x1, Pallas kernels, on_device(): pl.pallas_call(functools.partial(kernel, counts), out_shape=jax.ShapeDtyp...  23.1 us
    unnamed x1, local copies, waits for them, and re-layouts  0.67 us

profile of v1, /device:TPU:0, one launch (start us, length us, event | category | flops | bytes accessed | tf_op | source)
XLA Modules:
  0.0 23.8 jit_solution(8855189077547013941)
XLA Ops:
  0.0 23.1 %shard_map.55 = f32[320,128]{1,0:T(8,128)S(1)} custom-call(f32[5,8,8,128]{3,2,1,0:T(8,128)} %residual_hbm.1, f32[5,8,8,128]{3,2,1,0:T(8,128)} %flow_hbm.1, f32[3,5,8,8,128]{4,3,2,1,0:T(8,128)} %f_zeta_hbm.1, f32[15,64,128]{2,1,0:T(8,128)} %bitcast.4, f32[960,128]{1,0:T(8,128)} %bitcast.5), custom_call_target="tpu_custom_call" | custom-call | tf_op jit(solution)/shard_map/pallas_call | solution.py:893
  23.1 0.7 %copy.7 = f32[5,8,8,128]{3,2,1,0:T(8,128)} copy(f32[5,8,8,128]{3,2,1,0:T(8,128)S(1)} %bitcast.3) | data formatting | bytes 327680

commit v2 on v0

--- a/solution.py
+++ b/solution.py
@@ -576,20 +576,6 @@
     loads[3].wait()
     source[...] = residual[...] - dissipation * total_part
 
-    loads[2].wait()
-
-    for s in range(cx):
-        for k in range(5):
-            for g in range(3):
-                x_factors[k, s, g] = f_xi[pl.ds((g * 5 + k) * cz * cx + s, cz, stride=cx), :]
-
-    def xi_factor(k, s):
-        return x_factors[k, s]
-
-    def keep_x(s, now):
-        x_response[s] = now
-
-    xi.put_matrices(responses(cx, xi_factor, keep_x))
     zeta.join_matrices()
 
     for number, (x, slots, origin) in enumerate(halos):
@@ -632,6 +618,21 @@
         z_local.append(local)
     for h in range(len(streams)):
         zeta.solve(h)
+
+    loads[2].wait()
+
+    for s in range(cx):
+        for k in range(5):
+            for g in range(3):
+                x_factors[k, s, g] = f_xi[pl.ds((g * 5 + k) * cz * cx + s, cz, stride=cx), :]
+
+    def xi_factor(k, s):
+        return x_factors[k, s]
+
+    def keep_x(s, now):
+        x_response[s] = now
+
+    xi.put_matrices(responses(cx, xi_factor, keep_x))
 
     loads[4].wait()
     tiles = lines.shape[0] // cy
@@ -650,7 +651,6 @@
     def tiled(planes, at=slice(None)):
         return jnp.concatenate([planes[u : u + 1] for u in uses[at]], 0)
 
-    xi.join_matrices()
 
     def eta_factor(k, s):
         return e_factors[k, s]
@@ -667,6 +667,7 @@
     for c, values in enumerate(inner):
         for k in range(4):
             e_inner[k, :, :, c : c + 1, :] = values[k]
+    xi.join_matrices()
     e_msend[...] = jnp.concatenate([left[0][0:2], left[1][0:2], left[2], left[3]], 0)
     e_mslots[xe.me] = e_msend[...]
     xe.start(0, lambda p: e_msend, e_mslots)

time: 23.7 us -> 23.6 us (level)
  no operation moved by 1% of the time
where the time goes in v2:
time: 23.6 us; the launch traced here: 23.5 us
  Pallas kernels  22.8 us (97%)
  local copies, waits for them, and re-layouts  0.67 us (3%)
    pallas_call x1, Pallas kernels, on_device(): pl.pallas_call(functools.partial(kernel, counts), out_shape=jax.ShapeDtyp...  22.8 us
    unnamed x1, local copies, waits for them, and re-layouts  0.67 us

profile of v2, /device:TPU:0, one launch (start us, length us, event | category | flops | bytes accessed | tf_op | source)
XLA Modules:
  0.0 23.5 jit_solution(15434669349045131737)
XLA Ops:
  0.0 22.8 %shard_map.55 = f32[320,128]{1,0:T(8,128)S(1)} custom-call(f32[5,8,8,128]{3,2,1,0:T(8,128)} %residual_hbm.1, f32[5,8,8,128]{3,2,1,0:T(8,128)} %flow_hbm.1, f32[3,5,8,8,128]{4,3,2,1,0:T(8,128)} %f_zeta_hbm.1, f32[15,64,128]{2,1,0:T(8,128)} %bitcast.4, f32[960,128]{1,0:T(8,128)} %bitcast.5), custom_call_target="tpu_custom_call" | custom-call | tf_op jit(solution)/shard_map/pallas_call | solution.py:885
  22.8 0.7 %copy.7 = f32[5,8,8,128]{3,2,1,0:T(8,128)} copy(f32[5,8,8,128]{3,2,1,0:T(8,128)S(1)} %bitcast.3) | data formatting | bytes 327680

commit v3 on v0

--- a/solution.py
+++ b/solution.py
@@ -21,7 +21,7 @@
 
 
 def streams_of(per_tile):
-    return [own for own in (line_order[:per_tile], line_order[per_tile:]) if own]
+    return [line_order[k : k + per_tile] for k in range(0, len(line_order), per_tile)]
 
 
 def line_tiles(per_tile):

time: 23.7 us -> 23.7 us (level)
  no operation moved by 1% of the time
where the time goes in v3:
time: 23.7 us; the launch traced here: 23.6 us
  Pallas kernels  22.9 us (97%)
  local copies, waits for them, and re-layouts  0.67 us (3%)
    pallas_call x1, Pallas kernels, on_device(): pl.pallas_call(functools.partial(kernel, counts), out_shape=jax.ShapeDtyp...  22.9 us
    unnamed x1, local copies, waits for them, and re-layouts  0.67 us

profile of v3, /device:TPU:0, one launch (start us, length us, event | category | flops | bytes accessed | tf_op | source)
XLA Modules:
  0.0 23.6 jit_solution(11334972233930189342)
XLA Ops:
  0.0 22.9 %shard_map.55 = f32[320,128]{1,0:T(8,128)S(1)} custom-call(f32[5,8,8,128]{3,2,1,0:T(8,128)} %residual_hbm.1, f32[5,8,8,128]{3,2,1,0:T(8,128)} %flow_hbm.1, f32[3,5,8,8,128]{4,3,2,1,0:T(8,128)} %f_zeta_hbm.1, f32[15,64,128]{2,1,0:T(8,128)} %bitcast.4, f32[960,128]{1,0:T(8,128)} %bitcast.5), custom_call_target="tpu_custom_call" | custom-call | tf_op jit(solution)/shard_map/pallas_call | solution.py:884
  22.9 0.7 %copy.7 = f32[5,8,8,128]{3,2,1,0:T(8,128)} copy(f32[5,8,8,128]{3,2,1,0:T(8,128)S(1)} %bitcast.3) | data formatting | bytes 327680
